TPU v7x, 512 devices: a whole 4x4x16 slice. The times are simulated.
512 devices in a mesh: site: 16 (over z), bond: 32 (over y, x, core).
Axes of the slice: x: 4, y: 4, z: 16, core: 2. Of those that a mesh axis runs over, the one named last changes fastest.
Arguments:
- site_tensor: float32 [16, 4, 3072, 3072], P('site', None, 'bond'), may hold values from -0.21875 to 0.21875
- panels: float32 [16, 3072, 128], P('site', 'bond'), may hold values from -6 to 6
- fresh: float32 [1, 3072, 128], P(None, 'bond'), may hold values from -6 to 6
- outcomes: int32 [16, 2, 128], P('site'), may hold values from 0 to 3, as said below
Outputs:
- carried: float32 [16, 2, 3072, 128], P('site', None, 'bond')
Inputs may be any that keep to these rules, and one draw needn't show every extreme that they name: `outcomes`: at each site and tick, every outcome is taken by at most 48 samples, and some outcome by exactly 48.
All inputs are finite; a program needn't handle non-finite values.
Results may differ from a plain program's by a relative error of at most 0.0001.
Values sent between devices are 32-bit elements; how exact they have to be, the bound alone decides.
No kernel may reach another device: no remote copies, remote signals or barrier semaphores. Data moves between devices by JAX's collectives and lax.ppermute only.
A program may use at most 64 MiB of HBM per device.

v0:
```python
import jax
import jax.numpy as jnp
from jax import lax
from jax.sharding import PartitionSpec as P

TICKS = 2


def from_behind(value, axis, steps):
    count = lax.axis_size(axis)
    initial, last = (max(0, -steps), min(count, count - steps))
    return lax.ppermute(value, axis, [(source, source + steps) for source in range(initial, last)])


def contribute(tensor, vectors, selected):
    outcome_count = tensor.shape[0]
    chosen = (selected[None, :] == jnp.arange(outcome_count, dtype=jnp.int32)[:, None]).astype(
        jnp.float32
    )
    products = lax.dot_general(
        tensor,
        vectors,
        (((1,), (0,)), ((), ())),
        precision=lax.Precision.HIGHEST,
        preferred_element_type=jnp.float32,
    )
    return jnp.sum(products * chosen[:, None, :], axis=0)


def advance(tensor, vectors, selected):
    rows_local = tensor.shape[1]
    complete = contribute(tensor, vectors, selected)
    summed = lax.psum(complete, "bond")
    bond_index = lax.axis_index("bond")
    return lax.dynamic_slice_in_dim(summed, bond_index * rows_local, rows_local, 0)


def on_device(site_tensor, panels, fresh, outcomes):
    tensor = site_tensor[0]
    current = panels[0]
    results = []
    for tick_index in range(TICKS):
        produced = advance(tensor, current, outcomes[0, tick_index])
        results.append(produced)
        if tick_index + 1 < TICKS:
            passed = from_behind(produced, "site", 1)
            current = jnp.where(lax.axis_index("site") == 0, fresh[tick_index], passed)
    return jnp.stack(results, 0)[None]


def solution(mesh):
    placed = (
        P("site", None, "bond", None),
        P("site", "bond", None),
        P(None, "bond", None),
        P("site", None, None),
    )
    return jax.shard_map(
        on_device,
        mesh=mesh,
        in_specs=placed,
        out_specs=P("site", None, "bond", None),
        check_vma=False,
    )
```

profile of v0, /device:TPU:6, one launch (start us, length us, event | category | flops | bytes accessed | tf_op | source)
XLA Modules:
  0.0 324.4 jit_solution(2614767855735934217)
XLA Ops:
  6.5 0.0 copy-start
  6.5 0.0 copy-start.1
  6.5 0.0 all-reduce.3.cloned.1.call-start
  6.5 0.8 slice_bitcast_fusion.1
  7.3 0.1 copy-done
  7.4 13.1 %multiply_reduce_fusion = f32[3072,128]{1,0:T(8,128)} fusion(f32[1,4,96,3072]{3,2,1,0:T(8,128)} %param.4, f32[4,128]{1,0:T(4,128)S(1)} %fusion.6, f32[1,96,128]{2,1,0:T(8,128)S(1)} %copy-done), kind=kOutput, calls=%fused_computation.2 | convolution fusion | flops 1814691840 | bytes 6342656 | tf_op jit(solution)/shard_map/dot_general | solution.py:20
  20.4 0.0 all-reduce.3.cloned.1.call-update
  20.4 0.0 all-reduce.5.cloned.1.call-start
  20.5 142.2 %all-reduce.3.cloned.1.call-done = f32[3072,128]{1,0:T(8,128)} async-done(((f32[3072,128]{1,0:T(8,128)}), f32[3072,128]{1,0:T(8,128)}) %all-reduce.3.cloned.1.call-update) | async-done | bytes 1572880 | tf_op jit(solution)/shard_map/psum | solution.py:33
  162.7 0.8 constant_dynamic-slice_fusion.1
  163.5 3.4 %collective-permute-start = (f32[96,128]{1,0:T(8,128)S(1)}, f32[96,128]{1,0:T(8,128)S(1)}, u32[]{:S(2)}, u32[]{:S(2)}) collective-permute-start(f32[96,128]{1,0:T(8,128)S(1)} %constant_dynamic-slice_fusion.1), channel_id=1, source_target_pairs={{0,32},{32,64},{64,96},{96,128},{128,160},{160,192},{192,224},{224... | collective-permute-start | bytes 147464 | tf_op jit(solution)/shard_map/ppermute | solution.py:12
  167.0 1.7 collective-permute-done
  168.7 0.0 copy-done.1
  168.7 8.6 %fusion = f32[3072,128]{0,1:T(8,128)} fusion(f32[1,4,96,3072]{3,2,1,0:T(8,128)} %param.4, f32[4,128]{1,0:T(4,128)S(1)} %fusion.7, f32[96,128]{1,0:T(8,128)S(1)} %collective-permute-done, f32[1,96,128]{2,1,0:T(8,128)S(1)} %copy-done.1, pred[]{:T(512)S(6)} %eq.45), kind=kOutput, calls=%fused_computation.1 | convolution fusion | flops 1814704128 | bytes 6391809 | tf_op jit(solution)/shard_map/dot_general | solution.py:20
  177.3 0.0 all-reduce.5.cloned.1.call-update
  177.4 0.8 fusion.8
  178.2 137.6 %all-reduce.5.cloned.1.call-done = f32[3072,128]{0,1:T(8,128)} async-done(((f32[3072,128]{0,1:T(8,128)}), f32[3072,128]{0,1:T(8,128)}) %all-reduce.5.cloned.1.call-update) | async-done | bytes 1572880 | tf_op jit(solution)/shard_map/psum | solution.py:33
  315.8 1.0 constant_dynamic-slice_fusion
  316.8 0.1 copy.5
  316.9 0.7 maximum_bitcast_fusion
  (2 shorter events, 0.0 us)
Async XLA Ops:
  6.5 0.8 copy-start
  6.5 162.2 %copy-start.1 = (f32[1,96,128]{2,1,0:T(8,128)S(1)}, f32[1,96,128]{2,1,0:T(8,128)}, u32[]{:S(2)}) copy-start(f32[1,96,128]{2,1,0:T(8,128)} %param.6) | copy-start | bytes 147460
  6.5 156.2 %all-reduce.3.cloned.1.call-start = ((), (), s32[]{:S(2)}) async-start(), calls=%async_computation | async-start | bytes 3145728 | tf_op jit(solution)/shard_map/psum | solution.py:33
  20.4 295.4 %all-reduce.5.cloned.1.call-start = ((), (), s32[]{:S(2)}) async-start(), calls=%async_computation.1 | async-start | bytes 3145728 | tf_op jit(solution)/shard_map/psum | solution.py:33
  163.5 5.2 %collective-permute-start = (f32[96,128]{1,0:T(8,128)S(1)}, f32[96,128]{1,0:T(8,128)S(1)}, u32[]{:S(2)}, u32[]{:S(2)}) collective-permute-start(f32[96,128]{1,0:T(8,128)S(1)} %constant_dynamic-slice_fusion.1), channel_id=1, source_target_pairs={{0,32},{32,64},{64,96},{96,128},{128,160},{160,192},{192,224},{224... | collective-permute-start | bytes 147464 | tf_op jit(solution)/shard_map/ppermute | solution.py:12
Sparse Core Ops, SparseCore 0:
  20.6 142.1 all-reduce.2
  177.5 138.2 all-reduce.4
where the time goes:
time: 325 us; the launch traced here: 324 us
  waiting for transfers between devices  282 us (87%)
  matrix products  21.7 us (7%)
  between operations  13.4 us (4%)
  local copies, waits for them, and re-layouts  3.5 us (1%)
  starting transfers between devices  3.49 us (1%)
    psum x2, waiting for transfers between devices, advance(): summed = lax.psum(complete, 'bond')  280 us
    dot_general x2, matrix products, contribute(): lax.dot_general(tensor, vectors, (((1,), (0,)), ((), ())), precision=lax....  21.7 us
  transfers between devices with their start and end apart: 3, of which 3 were waited for; matrix products, arithmetic and copies ran while one was open for 0% of the time, Pallas kernels for 0%

commit v1 on v0

--- a/solution.py
+++ b/solution.py
@@ -30,7 +30,11 @@
 def advance(tensor, vectors, selected):
     rows_local = tensor.shape[1]
     complete = contribute(tensor, vectors, selected)
-    summed = lax.psum(complete, "bond")
+    n_dev = lax.axis_size("bond")
+    summed, stride = (complete, 1)
+    while stride < n_dev:
+        summed = summed + lax.ppermute(summed, "bond", [(i, i ^ stride) for i in range(n_dev)])
+        stride = 2 * stride
     bond_index = lax.axis_index("bond")
     return lax.dynamic_slice_in_dim(summed, bond_index * rows_local, rows_local, 0)
 

time: 325 us -> 345 us (1.062)
  starting transfers between devices: 3.49 us -> 31.9 us
  between operations: 13.4 us -> 0.19 us
  waiting for transfers between devices: 282 us -> 288 us
    ppermute x0 -> x10, waiting for transfers between devices: none -> 286 us  [advance(): lax.ppermute(summed, 'bond', [(i, i ^ stride) for i in range(n_dev)])]
    psum x2 -> x0, waiting for transfers between devices: 280 us -> none  [advance(): summed = lax.psum(complete, 'bond')]
    ppermute x0 -> x10, starting transfers between devices: none -> 30.7 us  [advance(): lax.ppermute(summed, 'bond', [(i, i ^ stride) for i in range(n_dev)])]
  transfers between devices with their start and end apart: 3 -> 11, of which waited for: 3 -> 11; matrix products, arithmetic and copies ran while one was open for 0% -> 0% of each run, Pallas kernels for 0% -> 0%
where the time goes in v1:
time: 345 us; the launch traced here: 343 us
  waiting for transfers between devices  288 us (83%)
  starting transfers between devices  31.9 us (9%)
  matrix products  19.5 us (6%)
    ppermute x10, waiting for transfers between devices, advance(): lax.ppermute(summed, 'bond', [(i, i ^ stride) for i in range(n_dev)])  286 us
    ppermute x10, starting transfers between devices, advance(): lax.ppermute(summed, 'bond', [(i, i ^ stride) for i in range(n_dev)])  30.7 us
    dot_general x2, matrix products, contribute(): lax.dot_general(tensor, vectors, (((1,), (0,)), ((), ())), precision=lax....  19.5 us
  transfers between devices with their start and end apart: 11, of which 11 were waited for; matrix products, arithmetic and copies ran while one was open for 0% of the time, Pallas kernels for 0%

profile of v1, /device:TPU:6, one launch (start us, length us, event | category | flops | bytes accessed | tf_op | source)
XLA Modules:
  0.0 342.6 jit_solution(9482945624864605307)
XLA Ops:
  0.8 11.9 %multiply_reduce_fusion = f32[3072,128]{1,0:T(8,128)S(1)} fusion(f32[1,4,96,3072]{3,2,1,0:T(8,128)} %param.4, f32[4,128]{1,0:T(4,128)S(1)} %fusion.6, f32[1,96,128]{2,1,0:T(8,128)S(1)} %copy-done), kind=kOutput, calls=%fused_computation.2 | convolution fusion | flops 1814691840 | bytes 6342656 | tf_op jit(solution)/shard_map/dot_general | solution.py:20
  12.8 1.9 collective-permute-start
  14.7 3.4 collective-permute-done
  18.3 2.7 collective-permute-start.1
  21.0 35.6 %collective-permute-done.1 = f32[3072,128]{1,0:T(8,128)S(1)} collective-permute-done((f32[3072,128]{1,0:T(8,128)S(1)}, f32[3072,128]{1,0:T(8,128)S(1)}, u32[]{:S(2)}, u32[]{:S(2)}) %collective-permute-start.1) | collective-permute-done | bytes 1572896 | tf_op jit(solution)/shard_map/ppermute | solution.py:36
  56.8 7.5 %collective-permute-start.2 = (f32[3072,128]{1,0:T(8,128)S(1)}, f32[3072,128]{1,0:T(8,128)S(1)}, u32[]{:S(2)}, u32[]{:S(2)}) collective-permute-start(f32[3072,128]{1,0:T(8,128)S(1)} %add.35), channel_id=1, source_target_pairs={{0,4},{1,5},{2,6},{3,7},{4,0},{5,1},{6,2},{7,3},{8,12},{9,13},{10,... | collective-permute-start | bytes 4718600 | tf_op jit(solution)/shard_map/ppermute | solution.py:36
  64.3 34.2 %collective-permute-done.2 = f32[3072,128]{1,0:T(8,128)S(1)} collective-permute-done((f32[3072,128]{1,0:T(8,128)S(1)}, f32[3072,128]{1,0:T(8,128)S(1)}, u32[]{:S(2)}, u32[]{:S(2)}) %collective-permute-start.2) | collective-permute-done | bytes 1572896 | tf_op jit(solution)/shard_map/ppermute | solution.py:36
  98.6 2.1 collective-permute-start.3
  100.7 35.3 %collective-permute-done.3 = f32[3072,128]{1,0:T(8,128)S(1)} collective-permute-done((f32[3072,128]{1,0:T(8,128)S(1)}, f32[3072,128]{1,0:T(8,128)S(1)}, u32[]{:S(2)}, u32[]{:S(2)}) %collective-permute-start.3) | collective-permute-done | bytes 1572896 | tf_op jit(solution)/shard_map/ppermute | solution.py:36
  136.2 1.9 collective-permute-start.4
  138.1 35.9 %collective-permute-done.4 = f32[3072,128]{1,0:T(8,128)S(1)} collective-permute-done((f32[3072,128]{1,0:T(8,128)S(1)}, f32[3072,128]{1,0:T(8,128)S(1)}, u32[]{:S(2)}, u32[]{:S(2)}) %collective-permute-start.4) | collective-permute-done | bytes 1572896 | tf_op jit(solution)/shard_map/ppermute | solution.py:36
  174.0 1.3 collective-permute-start.5
  175.3 1.7 collective-permute-done.5
  177.0 7.6 %fusion = f32[3072,128]{0,1:T(8,128)S(1)} fusion(f32[1,4,96,3072]{3,2,1,0:T(8,128)} %param.4, f32[4,128]{1,0:T(4,128)S(1)} %fusion.7, f32[96,128]{1,0:T(8,128)S(1)} %collective-permute-done.5, f32[1,96,128]{2,1,0:T(8,128)S(1)} %copy-done.1, pred[]{:T(512)S(6)} %eq.45), kind=kOutput, calls=%fused_computation.1 | convolution fusion | flops 1814704128 | bytes 6391809 | tf_op jit(solution)/shard_map/dot_general | solution.py:20
  184.6 1.9 collective-permute-start.6
  186.5 3.4 collective-permute-done.6
  190.1 2.0 collective-permute-start.7
  192.1 36.3 %collective-permute-done.7 = f32[3072,128]{0,1:T(8,128)S(1)} collective-permute-done((f32[3072,128]{0,1:T(8,128)S(1)}, f32[3072,128]{0,1:T(8,128)S(1)}, u32[]{:S(2)}, u32[]{:S(2)}) %collective-permute-start.7) | collective-permute-done | bytes 1572896 | tf_op jit(solution)/shard_map/ppermute | solution.py:36
  228.6 4.5 %collective-permute-start.8 = (f32[3072,128]{0,1:T(8,128)S(1)}, f32[3072,128]{0,1:T(8,128)S(1)}, u32[]{:S(2)}, u32[]{:S(2)}) collective-permute-start(f32[3072,128]{0,1:T(8,128)S(1)} %add.41), channel_id=1, source_target_pairs={{0,4},{1,5},{2,6},{3,7},{4,0},{5,1},{6,2},{7,3},{8,12},{9,13},{10,... | collective-permute-start | bytes 4718600 | tf_op jit(solution)/shard_map/ppermute | solution.py:36
  233.1 34.5 %collective-permute-done.8 = f32[3072,128]{0,1:T(8,128)S(1)} collective-permute-done((f32[3072,128]{0,1:T(8,128)S(1)}, f32[3072,128]{0,1:T(8,128)S(1)}, u32[]{:S(2)}, u32[]{:S(2)}) %collective-permute-start.8) | collective-permute-done | bytes 1572896 | tf_op jit(solution)/shard_map/ppermute | solution.py:36
  267.8 2.5 collective-permute-start.9
  270.3 34.1 %collective-permute-done.9 = f32[3072,128]{0,1:T(8,128)S(1)} collective-permute-done((f32[3072,128]{0,1:T(8,128)S(1)}, f32[3072,128]{0,1:T(8,128)S(1)}, u32[]{:S(2)}, u32[]{:S(2)}) %collective-permute-start.9) | collective-permute-done | bytes 1572896 | tf_op jit(solution)/shard_map/ppermute | solution.py:36
  304.6 3.7 %collective-permute-start.10 = (f32[3072,128]{0,1:T(8,128)S(1)}, f32[3072,128]{0,1:T(8,128)S(1)}, u32[]{:S(2)}, u32[]{:S(2)}) collective-permute-start(f32[3072,128]{0,1:T(8,128)S(1)} %add.43), channel_id=1, source_target_pairs={{0,16},{1,17},{2,18},{3,19},{4,20},{5,21},{6,22},{7,23},{8,24},{9,... | collective-permute-start | bytes 4718600 | tf_op jit(solution)/shard_map/ppermute | solution.py:36
  308.3 33.5 %collective-permute-done.10 = f32[3072,128]{0,1:T(8,128)S(1)} collective-permute-done((f32[3072,128]{0,1:T(8,128)S(1)}, f32[3072,128]{0,1:T(8,128)S(1)}, u32[]{:S(2)}, u32[]{:S(2)}) %collective-permute-start.10) | collective-permute-done | bytes 1572896 | tf_op jit(solution)/shard_map/ppermute | solution.py:36
  (19 shorter events, 3.1 us)
Async XLA Ops:
  0.0 0.8 copy-start
  12.8 5.3 %collective-permute-start = (f32[3072,128]{1,0:T(8,128)S(1)}, f32[3072,128]{1,0:T(8,128)S(1)}, u32[]{:S(2)}, u32[]{:S(2)}) collective-permute-start(f32[3072,128]{1,0:T(8,128)S(1)} %multiply_reduce_fusion), channel_id=1, source_target_pairs={{0,1},{1,0},{2,3},{3,2},{4,5},{5,4},{6,7},{7,6},{8,9},{9,8},{10,11... | collective-permute-start | bytes 4718600 | tf_op jit(solution)/shard_map/ppermute | solution.py:36
  18.3 38.3 %collective-permute-start.1 = (f32[3072,128]{1,0:T(8,128)S(1)}, f32[3072,128]{1,0:T(8,128)S(1)}, u32[]{:S(2)}, u32[]{:S(2)}) collective-permute-start(f32[3072,128]{1,0:T(8,128)S(1)} %add.34), channel_id=1, source_target_pairs={{0,2},{1,3},{2,0},{3,1},{4,6},{5,7},{6,4},{7,5},{8,10},{9,11},{10,... | collective-permute-start | bytes 4718600 | tf_op jit(solution)/shard_map/ppermute | solution.py:36
  56.8 41.7 %collective-permute-start.2 = (f32[3072,128]{1,0:T(8,128)S(1)}, f32[3072,128]{1,0:T(8,128)S(1)}, u32[]{:S(2)}, u32[]{:S(2)}) collective-permute-start(f32[3072,128]{1,0:T(8,128)S(1)} %add.35), channel_id=1, source_target_pairs={{0,4},{1,5},{2,6},{3,7},{4,0},{5,1},{6,2},{7,3},{8,12},{9,13},{10,... | collective-permute-start | bytes 4718600 | tf_op jit(solution)/shard_map/ppermute | solution.py:36
  98.6 78.4 %copy-start.1 = (f32[1,96,128]{2,1,0:T(8,128)S(1)}, f32[1,96,128]{2,1,0:T(8,128)}, u32[]{:S(2)}) copy-start(f32[1,96,128]{2,1,0:T(8,128)} %param.6) | copy-start | bytes 147460
  98.6 37.4 %collective-permute-start.3 = (f32[3072,128]{1,0:T(8,128)S(1)}, f32[3072,128]{1,0:T(8,128)S(1)}, u32[]{:S(2)}, u32[]{:S(2)}) collective-permute-start(f32[3072,128]{1,0:T(8,128)S(1)} %add.36), channel_id=1, source_target_pairs={{0,8},{1,9},{2,10},{3,11},{4,12},{5,13},{6,14},{7,15},{8,0},{9,1},... | collective-permute-start | bytes 4718600 | tf_op jit(solution)/shard_map/ppermute | solution.py:36
  136.2 37.8 %collective-permute-start.4 = (f32[3072,128]{1,0:T(8,128)S(1)}, f32[3072,128]{1,0:T(8,128)S(1)}, u32[]{:S(2)}, u32[]{:S(2)}) collective-permute-start(f32[3072,128]{1,0:T(8,128)S(1)} %add.37), channel_id=1, source_target_pairs={{0,16},{1,17},{2,18},{3,19},{4,20},{5,21},{6,22},{7,23},{8,24},{9,... | collective-permute-start | bytes 4718600 | tf_op jit(solution)/shard_map/ppermute | solution.py:36
  174.0 3.0 collective-permute-start.5
  184.6 5.3 %collective-permute-start.6 = (f32[3072,128]{0,1:T(8,128)S(1)}, f32[3072,128]{0,1:T(8,128)S(1)}, u32[]{:S(2)}, u32[]{:S(2)}) collective-permute-start(f32[3072,128]{0,1:T(8,128)S(1)} %fusion), channel_id=1, source_target_pairs={{0,1},{1,0},{2,3},{3,2},{4,5},{5,4},{6,7},{7,6},{8,9},{9,8},{10,11... | collective-permute-start | bytes 4718600 | tf_op jit(solution)/shard_map/ppermute | solution.py:36
  190.1 38.3 %collective-permute-start.7 = (f32[3072,128]{0,1:T(8,128)S(1)}, f32[3072,128]{0,1:T(8,128)S(1)}, u32[]{:S(2)}, u32[]{:S(2)}) collective-permute-start(f32[3072,128]{0,1:T(8,128)S(1)} %add.40), channel_id=1, source_target_pairs={{0,2},{1,3},{2,0},{3,1},{4,6},{5,7},{6,4},{7,5},{8,10},{9,11},{10,... | collective-permute-start | bytes 4718600 | tf_op jit(solution)/shard_map/ppermute | solution.py:36
  228.6 39.0 %collective-permute-start.8 = (f32[3072,128]{0,1:T(8,128)S(1)}, f32[3072,128]{0,1:T(8,128)S(1)}, u32[]{:S(2)}, u32[]{:S(2)}) collective-permute-start(f32[3072,128]{0,1:T(8,128)S(1)} %add.41), channel_id=1, source_target_pairs={{0,4},{1,5},{2,6},{3,7},{4,0},{5,1},{6,2},{7,3},{8,12},{9,13},{10,... | collective-permute-start | bytes 4718600 | tf_op jit(solution)/shard_map/ppermute | solution.py:36
  267.8 36.6 %collective-permute-start.9 = (f32[3072,128]{0,1:T(8,128)S(1)}, f32[3072,128]{0,1:T(8,128)S(1)}, u32[]{:S(2)}, u32[]{:S(2)}) collective-permute-start(f32[3072,128]{0,1:T(8,128)S(1)} %add.42), channel_id=1, source_target_pairs={{0,8},{1,9},{2,10},{3,11},{4,12},{5,13},{6,14},{7,15},{8,0},{9,1},... | collective-permute-start | bytes 4718600 | tf_op jit(solution)/shard_map/ppermute | solution.py:36
  304.6 37.2 %collective-permute-start.10 = (f32[3072,128]{0,1:T(8,128)S(1)}, f32[3072,128]{0,1:T(8,128)S(1)}, u32[]{:S(2)}, u32[]{:S(2)}) collective-permute-start(f32[3072,128]{0,1:T(8,128)S(1)} %add.43), channel_id=1, source_target_pairs={{0,16},{1,17},{2,18},{3,19},{4,20},{5,21},{6,22},{7,23},{8,24},{9,... | collective-permute-start | bytes 4718600 | tf_op jit(solution)/shard_map/ppermute | solution.py:36
